TPU v7x, 256 devices: a whole 4x4x8 slice. The times are simulated.
256 devices in a mesh: seq: 256 (over z, y, x, core).
Axes of the slice: x: 4, y: 4, z: 8, core: 2. Of those that a mesh axis runs over, the one named last changes fastest.
Arguments:
- query_rows: bfloat16 [65536, 768], P('seq'), may hold values from -12 to 12
- key_rows: bfloat16 [65536, 768], P('seq'), may hold values from -12 to 12
- value_rows: bfloat16 [65536, 768], P('seq'), may hold values from -6 to 6
- grad_out: bfloat16 [65536, 768], P('seq'), may hold values from -6 to 6
- head_offset: int32 [3, 12], replicated, may hold values from 0 to 255, as said below
Outputs:
- attended: bfloat16 [65536, 768], P('seq')
- grad_query: bfloat16 [65536, 768], P('seq')
- grad_key: bfloat16 [65536, 768], P('seq')
- grad_value: bfloat16 [65536, 768], P('seq')
Inputs may be any that keep to these rules, and one draw needn't show every extreme that they name: `head_offset`: row l holds offsets from 0 to g * 1 - 1, with g = 4, 16, 256 for l = 0, 1, 2.
All inputs are finite; a program needn't handle non-finite values.
Results may differ from a plain program's by a relative error of at most 0.022.
Values may be sent and summed in bfloat16 or wider, within the bound.
A program may use at most 128 MiB of HBM per device.

v0:
```python
import jax
import jax.numpy as jnp
from jax import lax
from jax.experimental import pallas as pl
from jax.experimental.pallas import tpu as pltpu
from jax.sharding import PartitionSpec as P

HEADS = 12
HEAD_DIM = 64
TILE = 64
PAIRS = 3
HALF = 384
ROWS = 256
SCALE = HEAD_DIM**-0.5
SCALE2 = SCALE * 1.4426950408889634
FAR = 1e30
MESH = pl.DeviceIdType.MESH
SIB = 1
MASK_A = (2,)
MASK_B = (4, 8, 12)
MASK_C = (64, 128, 192)
F32 = jnp.float32
BF16 = jnp.bfloat16


def dot_nt(a, b):
    return lax.dot_general(a, b, (((1,), (1,)), ((), ())), preferred_element_type=F32)


def dot_nn(a, b):
    return lax.dot_general(a, b, (((1,), (0,)), ((), ())), preferred_element_type=F32)


def dot_tn(a, b):
    return lax.dot_general(a, b, (((0,), (0,)), ((), ())), preferred_element_type=F32)


def low_lanes(rows):
    return lax.broadcasted_iota(jnp.int32, (rows, 128), 1) < 64


def cat2(x):
    low = low_lanes(x.shape[0])
    zero = jnp.zeros_like(x)
    return jnp.concatenate([jnp.where(low, x, zero), jnp.where(low, zero, x)], axis=0)


def sel2(y):
    n = y.shape[0] // 2
    return jnp.where(low_lanes(n), y[:n], y[n:])


def stats_of(kk, vv, qc, gc):
    s = dot_nt(kk, qc) * SCALE2
    m = jnp.max(s, axis=0, keepdims=True)
    p = jnp.exp2(s - m)
    tot = jnp.sum(p, axis=0, keepdims=True)
    d = jnp.sum(p * dot_nt(vv, gc), axis=0, keepdims=True)
    return m, tot, d


def probs_of(kk, vv, qc, gc, lrow, drow):
    p = jnp.exp2(dot_nt(kk, qc) * SCALE2 - lrow)
    ds = (p * (dot_nt(vv, gc) - drow) * SCALE).astype(BF16)
    return p.astype(BF16), ds


def kernel(
    off, q_hbm, k_hbm, v_hbm, g_hbm,
    o_att, o_dq, o_dk, o_dv,
    xq, xk, xv, xg, ha, hb, hc, acc, stage, ca, cb, cc,
    lst, sta, stb, stc, ls, ea, eb, ec,
    in_sem, s1_send, s1_recv, x1_send, x1_recv, x2_send, x2_recv, out_sem, o_send, o_recv,
):
    me = lax.axis_index("seq")
    core = lax.rem(me, 2)
    other = 1 - core
    chip = me // 2
    masks = (SIB,) + MASK_A + MASK_B + MASK_C
    barrier = pltpu.get_barrier_semaphore()
    for m in masks:
        pl.semaphore_signal(barrier, inc=1, device_id=(me ^ m,), device_id_type=MESH)

    my_cols = pl.ds(pl.multiple_of(core * HALF, 128), HALF)
    sib_cols = pl.ds(pl.multiple_of(other * HALF, 128), HALF)
    my_rows = pl.ds(pl.multiple_of(core * ROWS, ROWS), ROWS)
    sib_rows = pl.ds(pl.multiple_of(other * ROWS, ROWS), ROWS)
    hbm = (k_hbm, v_hbm, q_hbm, g_hbm)
    xs = (xk, xv, xq, xg)
    loads = [
        pltpu.make_async_copy(h.at[:, my_cols], x.at[my_rows, :], in_sem.at[i])
        for i, (h, x) in enumerate(zip(hbm, xs))
    ]
    for c in loads:
        c.start()

    def head(level, j):
        return off[level, core * 6 + j]

    def live_b(j):
        o = head(1, j)
        return jnp.where(lax.rem(chip, 2) == o // 8, lax.rem(o, 8), -1)

    def live_c(j):
        o = head(2, j)
        return jnp.where(lax.rem(chip, 32) == o // 8, lax.rem(o, 8), -1)

    def local_stats(seg):
        rows = pl.ds(pl.multiple_of(seg * ROWS, ROWS), ROWS)

        def body(p, carry):
            cols = pl.ds(pl.multiple_of(p * 128, 128), 128)
            out = stats_of(xk[rows, cols], xv[rows, cols], cat2(xq[rows, cols]), cat2(xg[rows, cols]))
            for n, x in enumerate(out):
                for i in range(2):
                    lst[n, seg, pl.ds(2 * p + i, 1), :] = x[:, i * ROWS : (i + 1) * ROWS]
            return carry

        lax.fori_loop(0, PAIRS, body, 0)

    zero8 = jnp.zeros((8, ROWS), F32)
    for n in range(3):
        for s in range(2):
            lst[n, s] = zero8
        for st in (sta, stb, stc):
            st[n] = zero8[:, :128]

    for c in loads:
        c.wait()
    local_stats(core)
    pl.semaphore_wait(barrier, len(masks))

    def remote(src, dst, send, recv, mask):
        return pltpu.make_async_remote_copy(
            src_ref=src, dst_ref=dst, send_sem=send, recv_sem=recv,
            device_id=(me ^ mask,), device_id_type=MESH,
        )

    s1 = [
        remote(h.at[:, sib_cols], x.at[my_rows, :], s1_send.at[i], s1_recv.at[i], SIB)
        for i, (h, x) in enumerate(zip(hbm, xs))
    ]
    for c in s1:
        c.start()

    def pick(first):
        def body(p, carry):
            cols = pl.ds(pl.multiple_of(p * 128, 128), 128)
            low = lax.broadcasted_iota(jnp.int32, (1, 128), 1) < 64
            want_a = jnp.where(low, head(0, 2 * p), head(0, 2 * p + 1))
            want_b = jnp.where(low, lax.rem(head(1, 2 * p), 8), lax.rem(head(1, 2 * p + 1), 8))
            want_c = jnp.where(low, lax.rem(head(2, 2 * p), 8), lax.rem(head(2, 2 * p + 1), 8))

            def ones(want, count):
                return [jnp.where(want == t, 1.0, 0.0).astype(BF16) for t in range(count)]

            hot_a, hot_b, hot_c = ones(want_a, 4), ones(want_b, 8), ones(want_c, 8)

            def mix(tiles, hot):
                out = tiles[0] * hot[0]
                for tile, one in zip(tiles[1:], hot[1:]):
                    out += tile * one
                return out

            for n in (first, first + 1):
                tiles = [xs[n][pl.ds(t * TILE, TILE), cols] for t in range(8)]
                hc[n, 0, :, cols] = mix(tiles, hot_c)
                hb[n, 0, :, cols] = mix(tiles, hot_b)
                for s in range(2):
                    ha[n, s, :, cols] = mix(tiles[4 * s : 4 * s + 4], hot_a)
            return carry

        lax.fori_loop(0, PAIRS, body, 0)

    def send_tiles(half):
        two = pl.ds(2 * half, 2)
        base = 7 * half
        copies = []
        for i, m in enumerate(MASK_C):
            copies.append(remote(hc.at[two, 0], hc.at[two, i + 1], x1_send.at[base + i], x1_recv.at[base + i], m))
        for i, m in enumerate(MASK_B):
            copies.append(remote(hb.at[two, 0], hb.at[two, i + 1], x1_send.at[base + 3 + i], x1_recv.at[base + 3 + i], m))
        copies.append(
            remote(ha.at[two, pl.ds(0, 2)], ha.at[two, pl.ds(2, 2)], x1_send.at[base + 6], x1_recv.at[base + 6], MASK_A[0])
        )
        for c in copies:
            c.start()
        return copies

    s1[0].wait()
    s1[1].wait()
    pick(0)
    kv_copies = send_tiles(0)
    s1[2].wait()
    s1[3].wait()
    pick(2)
    qg_copies = send_tiles(1)
    local_stats(other)

    levels = ((ha, 2, sta, ca), (hb, 1, stb, cb), (hc, 1, stc, cc))

    def all_rows(h, n, cols):
        return h[n, :, :, cols].reshape(4 * TILE, 128)

    def own_rows(h, n, slots, cols):
        return h[n, pl.ds(0, slots), :, cols].reshape(slots * TILE, 128)

    def level_stats(h, slots, st):
        width = slots * TILE

        def body(p, carry):
            cols = pl.ds(pl.multiple_of(p * 128, 128), 128)
            out = stats_of(
                all_rows(h, 0, cols), all_rows(h, 1, cols),
                cat2(own_rows(h, 2, slots, cols)), cat2(own_rows(h, 3, slots, cols)),
            )
            for n, x in enumerate(out):
                for i in range(2):
                    st[n, pl.ds(2 * p + i, 1), pl.ds(0, width)] = x[:, i * width : (i + 1) * width]
            return carry

        lax.fori_loop(0, PAIRS, body, 0)

    kv_copies[6].wait()
    level_stats(ha, 2, sta)
    for c in kv_copies[3:6]:
        c.wait()
    level_stats(hb, 1, stb)
    for c in kv_copies[:3]:
        c.wait()
    level_stats(hc, 1, stc)

    row_id = lax.broadcasted_iota(jnp.int32, (8, ROWS), 0)
    lane_tile = lax.broadcasted_iota(jnp.int32, (8, ROWS), 1) // TILE

    def per_head(f, fill):
        out = jnp.full((8, ROWS), fill, jnp.int32)
        for j in range(6):
            out = jnp.where(row_id == j, f(j), out)
        return out

    tile_a = per_head(lambda j: head(0, j), 0)
    tile_b = per_head(live_b, -1)
    tile_c = per_head(live_c, -1)

    def rep4(x):
        return jnp.concatenate([x] * 4, axis=1)

    lse, delta = [], []
    for s in range(2):
        hits = (lane_tile == tile_a, lane_tile + 4 * s == tile_b, lane_tile + 4 * s == tile_c)
        parts = [tuple(lst[n, s] for n in range(3))]
        for hit, st, start in zip(hits, (sta, stb, stc), (s * TILE, 0, 0)):
            peak, tot, d = (rep4(st[n, :, pl.ds(start, TILE)]) for n in range(3))
            parts.append((jnp.where(hit, peak, -FAR), jnp.where(hit, tot, 0.0), jnp.where(hit, d, 0.0)))
        top = parts[0][0]
        for part in parts[1:]:
            top = jnp.maximum(top, part[0])
        total = jnp.zeros((8, ROWS), F32)
        dsum = jnp.zeros((8, ROWS), F32)
        for peak, tot, d in parts:
            factor = jnp.exp2(peak - top)
            total += tot * factor
            dsum += d * factor
        lse.append(top + jnp.log2(total))
        delta.append(dsum / total)
        ls[s, pl.ds(0, 8), :] = lse[s]
        ls[s, pl.ds(8, 8), :] = delta[s]

    def gather8(values, index, tiles):
        out = jnp.zeros((8, TILE), F32)
        for t in tiles:
            out = jnp.where(index[:, :TILE] == t % 8, values[t // 4 % 2][:, t % 4 * TILE : (t % 4 + 1) * TILE], out)
        return out

    for base, values in ((0, lse), (8, delta)):
        halves = []
        for s in range(2):
            out = jnp.zeros((8, TILE), F32)
            for t in range(4):
                out = jnp.where(tile_a[:, :TILE] == t, values[s][:, t * TILE : (t + 1) * TILE], out)
            halves.append(out)
        ea[0, pl.ds(base, 8), :] = jnp.concatenate(halves, axis=1)
        for e, index in ((eb, tile_b), (ec, tile_c)):
            out = gather8(values, index, range(8))
            if base == 0:
                out = jnp.where(index[:, :TILE] < 0, FAR, out)
            e[0, pl.ds(base, 8), :] = jnp.concatenate([out, out], axis=1)

    x2 = []
    for i, m in enumerate(MASK_C):
        x2.append(remote(ec.at[0], ec.at[i + 1], x2_send.at[i], x2_recv.at[i], m))
    for i, m in enumerate(MASK_B):
        x2.append(remote(eb.at[0], eb.at[i + 1], x2_send.at[3 + i], x2_recv.at[3 + i], m))
    x2.append(remote(ea.at[0], ea.at[1], x2_send.at[6], x2_recv.at[6], MASK_A[0]))
    for c in x2:
        c.start()

    low_row = lax.broadcasted_iota(jnp.int32, (1, 128), 1) < 64

    def local_back(n, carry):
        seg, p = n // PAIRS, lax.rem(n, PAIRS)
        rows = pl.ds(pl.multiple_of(seg * ROWS, ROWS), ROWS)
        cols = pl.ds(pl.multiple_of(p * 128, 128), 128)
        kk, vv = xk[rows, cols], xv[rows, cols]
        qc, gc = cat2(xq[rows, cols]), cat2(xg[rows, cols])
        lrow = jnp.concatenate([ls[seg, pl.ds(2 * p + i, 1), :] for i in range(2)], axis=1)
        drow = jnp.concatenate([ls[seg, pl.ds(8 + 2 * p + i, 1), :] for i in range(2)], axis=1)
        pb, ds = probs_of(kk, vv, qc, gc, lrow, drow)
        acc[0, rows, cols] = sel2(dot_tn(pb, vv))
        acc[1, rows, cols] = sel2(dot_tn(ds, kk))
        acc[2, rows, cols] = dot_nn(ds, qc)
        acc[3, rows, cols] = dot_nn(pb, gc)
        return carry

    lax.fori_loop(0, 2 * PAIRS, local_back, 0)

    def level_query(h, slots, e, c):
        def body(p, carry):
            cols = pl.ds(pl.multiple_of(p * 128, 128), 128)
            kk, vv = all_rows(h, 0, cols), all_rows(h, 1, cols)
            qc, gc = cat2(own_rows(h, 2, slots, cols)), cat2(own_rows(h, 3, slots, cols))
            rows = []
            for base in (0, 8):
                r0, r1 = (e[0, pl.ds(base + 2 * p + i, 1), :] for i in range(2))
                rows.append(jnp.concatenate([r0, r1], axis=1) if slots == 2 else jnp.where(low_row, r0, r1))
            pb, ds = probs_of(kk, vv, qc, gc, *rows)
            c[0, :, cols] = sel2(dot_tn(pb, vv))
            c[1, :, cols] = sel2(dot_tn(ds, kk))
            return carry

        lax.fori_loop(0, PAIRS, body, 0)

    def level_key(h, slots, e, c):
        n = slots * TILE

        def body(p, carry):
            cols = pl.ds(pl.multiple_of(p * 128, 128), 128)
            qq, gg = all_rows(h, 2, cols), all_rows(h, 3, cols)
            kc, vc = cat2(own_rows(h, 0, slots, cols)), cat2(own_rows(h, 1, slots, cols))

            def stat_row(r):
                if slots == 2:
                    return jnp.concatenate([e[0, pl.ds(r, 1), :], e[1, pl.ds(r, 1), :]], axis=1)
                s = [e[i, pl.ds(r, 1), :] for i in range(4)]
                return jnp.concatenate([jnp.where(low_row, s[0], s[1]), jnp.where(low_row, s[2], s[3])], axis=1)

            sc = dot_nt(kc, qq) * SCALE2
            dp = dot_nt(vc, gg)
            pbs, dss = [], []
            for i in range(2):
                part = slice(i * n, (i + 1) * n)
                pr = jnp.exp2(sc[part] - stat_row(2 * p + i))
                dss.append((pr * (dp[part] - stat_row(8 + 2 * p + i)) * SCALE).astype(BF16))
                pbs.append(pr.astype(BF16))
            c[2, :, cols] = sel2(dot_nn(jnp.concatenate(dss, axis=0), qq))
            c[3, :, cols] = sel2(dot_nn(jnp.concatenate(pbs, axis=0), gg))
            return carry

        lax.fori_loop(0, PAIRS, body, 0)

    def finish(outs):
        def body(p, carry):
            cols = pl.ds(pl.multiple_of(p * 128, 128), 128)
            low = low_lanes(TILE)
            pick_a = jnp.where(low, head(0, 2 * p), head(0, 2 * p + 1))
            pick_b = jnp.where(low, live_b(2 * p), live_b(2 * p + 1))
            pick_c = jnp.where(low, live_c(2 * p), live_c(2 * p + 1))
            for o in outs:
                b, c = cb[o, :, cols], cc[o, :, cols]
                for t in range(8):
                    rows = pl.ds(t * TILE, TILE)
                    a = ca[o, pl.ds(t // 4 * TILE, TILE), cols]
                    total = acc[o, rows, cols] + jnp.where(pick_a == t % 4, a, 0.0)
                    total += jnp.where(pick_b == t, b, 0.0)
                    total += jnp.where(pick_c == t, c, 0.0)
                    stage[o, rows, cols] = total.astype(BF16)
            return carry

        lax.fori_loop(0, PAIRS, body, 0)

    o_refs = (o_att, o_dq, o_dk, o_dv)

    def put(outs):
        copies = []
        for o in outs:
            copies.append(remote(stage.at[o, sib_rows, :], o_refs[o].at[:, my_cols], o_send.at[o], o_recv.at[o], SIB))
        for o in outs:
            copies.append(pltpu.make_async_copy(stage.at[o, my_rows, :], o_refs[o].at[:, my_cols], out_sem.at[o]))
        for c in copies:
            c.start()
        return copies

    es = (ea, eb, ec)
    for (h, slots, _, c), e in zip(levels, es):
        level_query(h, slots, e, c)
    finish((0, 1))
    final = put((0, 1))
    waits = ((6, 7), (3, 6), (0, 3))
    for (h, slots, _, c), e, (lo, hi) in zip(levels, es, waits):
        for i in range(lo, hi):
            qg_copies[i].wait()
            x2[i].wait()
        level_key(h, slots, e, c)
    finish((2, 3))
    final += put((2, 3))
    for c in final:
        c.wait()


def local(query_rows, key_rows, value_rows, grad_out, head_offset):
    rows = jax.ShapeDtypeStruct((ROWS, 2 * HALF), BF16)
    any_spec = pl.BlockSpec(memory_space=pl.ANY)
    dma = pltpu.SemaphoreType.DMA
    tile4 = pltpu.VMEM((4, 4, TILE, HALF), BF16)
    return pl.pallas_call(
        kernel,
        out_shape=[rows] * 4,
        in_specs=[pl.BlockSpec(memory_space=pltpu.SMEM)] + [any_spec] * 4,
        out_specs=[any_spec] * 4,
        scratch_shapes=[pltpu.VMEM((2 * ROWS, HALF), BF16)] * 4
        + [tile4] * 3
        + [
            pltpu.VMEM((4, 2 * ROWS, HALF), F32),
            pltpu.VMEM((4, 2 * ROWS, HALF), BF16),
            pltpu.VMEM((4, 2 * TILE, HALF), F32),
            pltpu.VMEM((4, TILE, HALF), F32),
            pltpu.VMEM((4, TILE, HALF), F32),
            pltpu.VMEM((3, 2, 8, ROWS), F32),
            pltpu.VMEM((3, 8, 128), F32),
            pltpu.VMEM((3, 8, 128), F32),
            pltpu.VMEM((3, 8, 128), F32),
            pltpu.VMEM((2, 16, ROWS), F32),
            pltpu.VMEM((2, 16, 128), F32),
            pltpu.VMEM((4, 16, 128), F32),
            pltpu.VMEM((4, 16, 128), F32),
            dma((4,)), dma((4,)), dma((4,)), dma((14,)), dma((14,)), dma((7,)), dma((7,)), dma((4,)), dma((4,)), dma((4,)),
        ],
        compiler_params=pltpu.CompilerParams(
            collective_id=0, has_side_effects=True, vmem_limit_bytes=40 * 1024 * 1024
        ),
        cost_estimate=pl.CostEstimate(flops=2_000_000_000, bytes_accessed=3_200_000, transcendentals=3_000_000),
    )(head_offset, query_rows, key_rows, value_rows, grad_out)


def solution(mesh):
    return jax.shard_map(
        local,
        mesh=mesh,
        in_specs=(P("seq", None), P("seq", None), P("seq", None), P("seq", None), P()),
        out_specs=(P("seq", None), P("seq", None), P("seq", None), P("seq", None)),
        check_vma=False,
    )
```

profile of v0, /device:TPU:1, one launch (start us, length us, event | category | flops | bytes accessed | tf_op | source)
XLA Modules:
  0.0 52.2 jit_solution(4346657528630404385)
XLA Ops:
  0.6 0.0 copy-start
  0.6 1.0 %copy-done = bf16[256,768]{1,0:T(8,128)(2,1)S(1)} copy-done((bf16[256,768]{1,0:T(8,128)(2,1)S(1)}, bf16[256,768]{1,0:T(8,128)(2,1)}, u32[]{:S(2)}) %copy-start) | copy-done | bytes 393240
  1.6 0.0 copy-start.1
  1.6 1.0 %copy-done.1 = bf16[256,768]{1,0:T(8,128)(2,1)S(1)} copy-done((bf16[256,768]{1,0:T(8,128)(2,1)S(1)}, bf16[256,768]{1,0:T(8,128)(2,1)}, u32[]{:S(2)}) %copy-start.1) | copy-done | bytes 393240
  2.6 0.0 copy-start.2
  2.6 1.0 %copy-done.2 = bf16[256,768]{1,0:T(8,128)(2,1)S(1)} copy-done((bf16[256,768]{1,0:T(8,128)(2,1)S(1)}, bf16[256,768]{1,0:T(8,128)(2,1)}, u32[]{:S(2)}) %copy-start.2) | copy-done | bytes 393240
  3.6 0.0 copy-start.3
  3.6 1.0 %copy-done.3 = bf16[256,768]{1,0:T(8,128)(2,1)S(1)} copy-done((bf16[256,768]{1,0:T(8,128)(2,1)S(1)}, bf16[256,768]{1,0:T(8,128)(2,1)}, u32[]{:S(2)}) %copy-start.3) | copy-done | bytes 393240
  4.6 0.0 copy-start.4
  4.6 0.7 %copy-done.4 = s32[3,12]{1,0:T(4,128)S(1)} copy-done((s32[3,12]{1,0:T(4,128)S(1)}, s32[3,12]{1,0:T(4,128)}, u32[]{:S(2)}) %copy-start.4) | copy-done | bytes 168
  5.3 43.9 %shard_map.84 = (bf16[256,768]{1,0:T(8,128)(2,1)S(1)}, bf16[256,768]{1,0:T(8,128)(2,1)S(1)}, bf16[256,768]{1,0:T(8,128)(2,1)S(1)}, bf16[256,768]{1,0:T(8,128)(2,1)S(1)}) custom-call(s32[3,12]{1,0:T(4,128)S(1)} %copy-done.4, bf16[256,768]{1,0:T(8,128)(2,1)S(1)} %copy-done, bf16[256,768]{1,0:T(8,128)(2,1)S(1)} %copy-done.1, bf16[256,768]{1,0:T(8,128)(2,1)S(1)} %copy-done.2, ...), custom_call_target="tpu_custom_call" | custom-call | flops 2000000000 | bytes 3200000 | tf_op jit(solution)/shard_map/pallas_call | solution.py:416
  49.2 0.7 %copy.13 = bf16[256,768]{1,0:T(8,128)(2,1)} copy(bf16[256,768]{1,0:T(8,128)(2,1)S(1)} %get-tuple-element.8) | data formatting | bytes 786432
  49.9 0.7 %copy.14 = bf16[256,768]{1,0:T(8,128)(2,1)} copy(bf16[256,768]{1,0:T(8,128)(2,1)S(1)} %get-tuple-element.9) | data formatting | bytes 786432
  50.7 0.7 %copy.15 = bf16[256,768]{1,0:T(8,128)(2,1)} copy(bf16[256,768]{1,0:T(8,128)(2,1)S(1)} %get-tuple-element.10) | data formatting | bytes 786432
  51.4 0.7 %copy.16 = bf16[256,768]{1,0:T(8,128)(2,1)} copy(bf16[256,768]{1,0:T(8,128)(2,1)S(1)} %get-tuple-element.11) | data formatting | bytes 786432
Async XLA Ops:
  0.6 1.0 %copy-start = (bf16[256,768]{1,0:T(8,128)(2,1)S(1)}, bf16[256,768]{1,0:T(8,128)(2,1)}, u32[]{:S(2)}) copy-start(bf16[256,768]{1,0:T(8,128)(2,1)} %q_hbm.1) | copy-start | bytes 1179652
  1.6 1.0 %copy-start.1 = (bf16[256,768]{1,0:T(8,128)(2,1)S(1)}, bf16[256,768]{1,0:T(8,128)(2,1)}, u32[]{:S(2)}) copy-start(bf16[256,768]{1,0:T(8,128)(2,1)} %k_hbm.1) | copy-start | bytes 1179652
  2.6 1.0 %copy-start.2 = (bf16[256,768]{1,0:T(8,128)(2,1)S(1)}, bf16[256,768]{1,0:T(8,128)(2,1)}, u32[]{:S(2)}) copy-start(bf16[256,768]{1,0:T(8,128)(2,1)} %v_hbm.1) | copy-start | bytes 1179652
  3.6 1.0 %copy-start.3 = (bf16[256,768]{1,0:T(8,128)(2,1)S(1)}, bf16[256,768]{1,0:T(8,128)(2,1)}, u32[]{:S(2)}) copy-start(bf16[256,768]{1,0:T(8,128)(2,1)} %g_hbm.1) | copy-start | bytes 1179652
  4.6 0.7 %copy-start.4 = (s32[3,12]{1,0:T(4,128)S(1)}, s32[3,12]{1,0:T(4,128)}, u32[]{:S(2)}) copy-start(s32[3,12]{1,0:T(4,128)} %off.1) | copy-start | bytes 436
where the time goes:
time: 52.4 us; the launch traced here: 52.2 us
  Pallas kernels  43.9 us (84%)
  local copies, waits for them, and re-layouts  7.64 us (15%)
  between operations  0.65 us (1%)
    pallas_call x1, Pallas kernels, local(): pl.pallas_call(kernel, out_shape=[rows] * 4, in_specs=[pl.BlockSpec(memor...  43.9 us
    unnamed x14, local copies, waits for them, and re-layouts  7.64 us

commit v1 on v0

--- a/solution.py
+++ b/solution.py
@@ -55,22 +55,29 @@
     m = jnp.max(s, axis=0, keepdims=True)
     p = jnp.exp2(s - m)
     tot = jnp.sum(p, axis=0, keepdims=True)
-    d = jnp.sum(p * dot_nt(vv, gc), axis=0, keepdims=True)
-    return m, tot, d
-
-
-def probs_of(kk, vv, qc, gc, lrow, drow):
-    p = jnp.exp2(dot_nt(kk, qc) * SCALE2 - lrow)
-    ds = (p * (dot_nt(vv, gc) - drow) * SCALE).astype(BF16)
-    return p.astype(BF16), ds
+    dp = dot_nt(vv, gc)
+    d = jnp.sum(p * dp, axis=0, keepdims=True)
+    return (m, tot, d), p, dp
+
+
+def probs_of(p, dp, peak, lrow, drow):
+    p = p * jnp.exp2(peak - lrow)
+    return p.astype(BF16), (p * SCALE * (dp - drow)).astype(BF16)
+
+
+def dup_lanes(x, upper):
+    low = low_lanes(x.shape[0])
+    other = pltpu.roll(x, 64, 1)
+    return jnp.where(low, other, x) if upper else jnp.where(low, x, other)
 
 
 def kernel(
-    off, q_hbm, k_hbm, v_hbm, g_hbm,
+    off_hbm, q_hbm, k_hbm, v_hbm, g_hbm,
     o_att, o_dq, o_dk, o_dv,
-    xq, xk, xv, xg, ha, hb, hc, acc, stage, ca, cb, cc,
+    xq, xk, xv, xg, xkt, xvt, ha, hb, hc, acc, acct, stage, ca, cb, cc, cat, cbt, cct,
+    lp, ldp, ap, adp, bp, bdp, cp, cdp,
     lst, sta, stb, stc, ls, ea, eb, ec,
-    in_sem, s1_send, s1_recv, x1_send, x1_recv, x2_send, x2_recv, out_sem, o_send, o_recv,
+    off, off_sem, in_sem, s1_send, s1_recv, x1_send, x1_recv, x2_send, x2_recv, out_sem, o_send, o_recv,
 ):
     me = lax.axis_index("seq")
     core = lax.rem(me, 2)
@@ -91,8 +98,10 @@
         pltpu.make_async_copy(h.at[:, my_cols], x.at[my_rows, :], in_sem.at[i])
         for i, (h, x) in enumerate(zip(hbm, xs))
     ]
+    load_off = pltpu.make_async_copy(off_hbm, off, off_sem)
     for c in loads:
         c.start()
+    load_off.start()
 
     def head(level, j):
         return off[level, core * 6 + j]
@@ -110,13 +119,16 @@
 
         def body(p, carry):
             cols = pl.ds(pl.multiple_of(p * 128, 128), 128)
-            out = stats_of(xk[rows, cols], xv[rows, cols], cat2(xq[rows, cols]), cat2(xg[rows, cols]))
+            kk, vv = xk[rows, cols], xv[rows, cols]
+            out, lp[seg, p], ldp[seg, p] = stats_of(kk, vv, cat2(xq[rows, cols]), cat2(xg[rows, cols]))
+            xkt[seg, cols, :] = kk.T
+            xvt[seg, cols, :] = vv.T
             for n, x in enumerate(out):
                 for i in range(2):
                     lst[n, seg, pl.ds(2 * p + i, 1), :] = x[:, i * ROWS : (i + 1) * ROWS]
             return carry
 
-        lax.fori_loop(0, PAIRS, body, 0)
+        lax.fori_loop(0, PAIRS, body, 0, unroll=True)
 
     zero8 = jnp.zeros((8, ROWS), F32)
     for n in range(3):
@@ -127,6 +139,7 @@
 
     for c in loads:
         c.wait()
+    load_off.wait()
     local_stats(core)
     pl.semaphore_wait(barrier, len(masks))
 
@@ -170,7 +183,7 @@
                     ha[n, s, :, cols] = mix(tiles[4 * s : 4 * s + 4], hot_a)
             return carry
 
-        lax.fori_loop(0, PAIRS, body, 0)
+        lax.fori_loop(0, PAIRS, body, 0, unroll=True)
 
     def send_tiles(half):
         two = pl.ds(2 * half, 2)
@@ -197,7 +210,7 @@
     qg_copies = send_tiles(1)
     local_stats(other)
 
-    levels = ((ha, 2, sta, ca), (hb, 1, stb, cb), (hc, 1, stc, cc))
+    levels = ((ha, 2, sta, ca, cat, ap, adp), (hb, 1, stb, cb, cbt, bp, bdp), (hc, 1, stc, cc, cct, cp, cdp))
 
     def all_rows(h, n, cols):
         return h[n, :, :, cols].reshape(4 * TILE, 128)
@@ -205,12 +218,12 @@
     def own_rows(h, n, slots, cols):
         return h[n, pl.ds(0, slots), :, cols].reshape(slots * TILE, 128)
 
-    def level_stats(h, slots, st):
+    def level_stats(h, slots, st, c, ct, kp, kdp):
         width = slots * TILE
 
         def body(p, carry):
             cols = pl.ds(pl.multiple_of(p * 128, 128), 128)
-            out = stats_of(
+            out, kp[p], kdp[p] = stats_of(
                 all_rows(h, 0, cols), all_rows(h, 1, cols),
                 cat2(own_rows(h, 2, slots, cols)), cat2(own_rows(h, 3, slots, cols)),
             )
@@ -219,16 +232,16 @@
                     st[n, pl.ds(2 * p + i, 1), pl.ds(0, width)] = x[:, i * width : (i + 1) * width]
             return carry
 
-        lax.fori_loop(0, PAIRS, body, 0)
+        lax.fori_loop(0, PAIRS, body, 0, unroll=True)
 
     kv_copies[6].wait()
-    level_stats(ha, 2, sta)
+    level_stats(*levels[0])
     for c in kv_copies[3:6]:
         c.wait()
-    level_stats(hb, 1, stb)
+    level_stats(*levels[1])
     for c in kv_copies[:3]:
         c.wait()
-    level_stats(hc, 1, stc)
+    level_stats(*levels[2])
 
     row_id = lax.broadcasted_iota(jnp.int32, (8, ROWS), 0)
     lane_tile = lax.broadcasted_iota(jnp.int32, (8, ROWS), 1) // TILE
@@ -298,38 +311,50 @@
 
     low_row = lax.broadcasted_iota(jnp.int32, (1, 128), 1) < 64
 
+    def head_rows(ref, seg, r):
+        return jnp.concatenate([ref[seg, pl.ds(r + i, 1), :] for i in range(2)], axis=1)
+
     def local_back(n, carry):
-        seg, p = n // PAIRS, lax.rem(n, PAIRS)
+        seg, p = n // PAIRS, n % PAIRS
         rows = pl.ds(pl.multiple_of(seg * ROWS, ROWS), ROWS)
         cols = pl.ds(pl.multiple_of(p * 128, 128), 128)
-        kk, vv = xk[rows, cols], xv[rows, cols]
         qc, gc = cat2(xq[rows, cols]), cat2(xg[rows, cols])
-        lrow = jnp.concatenate([ls[seg, pl.ds(2 * p + i, 1), :] for i in range(2)], axis=1)
-        drow = jnp.concatenate([ls[seg, pl.ds(8 + 2 * p + i, 1), :] for i in range(2)], axis=1)
-        pb, ds = probs_of(kk, vv, qc, gc, lrow, drow)
-        acc[0, rows, cols] = sel2(dot_tn(pb, vv))
-        acc[1, rows, cols] = sel2(dot_tn(ds, kk))
-        acc[2, rows, cols] = dot_nn(ds, qc)
-        acc[3, rows, cols] = dot_nn(pb, gc)
+        peak = jnp.concatenate([lst[0, seg, pl.ds(2 * p + i, 1), :] for i in range(2)], axis=1)
+        pb, ds = probs_of(lp[seg, p], ldp[seg, p], peak, head_rows(ls, seg, 2 * p), head_rows(ls, seg, 8 + 2 * p))
+        for i in range(2):
+            d = pl.ds(pl.multiple_of(p * 128 + i * 64, 64), 64)
+            part = slice(i * ROWS, (i + 1) * ROWS)
+            acct[0, d, rows] = dot_nn(xvt[seg, d, :], pb[:, part])
+            acct[1, d, rows] = dot_nn(xkt[seg, d, :], ds[:, part])
+        acc[0, rows, cols] = dot_nn(ds, qc)
+        acc[1, rows, cols] = dot_nn(pb, gc)
         return carry
 
-    lax.fori_loop(0, 2 * PAIRS, local_back, 0)
-
-    def level_query(h, slots, e, c):
-        def body(p, carry):
-            cols = pl.ds(pl.multiple_of(p * 128, 128), 128)
-            kk, vv = all_rows(h, 0, cols), all_rows(h, 1, cols)
-            qc, gc = cat2(own_rows(h, 2, slots, cols)), cat2(own_rows(h, 3, slots, cols))
-            rows = []
-            for base in (0, 8):
-                r0, r1 = (e[0, pl.ds(base + 2 * p + i, 1), :] for i in range(2))
-                rows.append(jnp.concatenate([r0, r1], axis=1) if slots == 2 else jnp.where(low_row, r0, r1))
-            pb, ds = probs_of(kk, vv, qc, gc, *rows)
-            c[0, :, cols] = sel2(dot_tn(pb, vv))
-            c[1, :, cols] = sel2(dot_tn(ds, kk))
-            return carry
-
-        lax.fori_loop(0, PAIRS, body, 0)
+    def level_query(h, slots, st, ct, kp, kdp, e):
+        def body(p, carry):
+            cols = pl.ds(pl.multiple_of(p * 128, 128), 128)
+            kt, vt = all_rows(h, 0, cols).T, all_rows(h, 1, cols).T
+
+            def pair(r0, r1):
+                return jnp.concatenate([r0, r1], axis=1) if slots == 2 else jnp.where(low_row, r0, r1)
+
+            lrow = pair(*(e[0, pl.ds(2 * p + i, 1), :] for i in range(2)))
+            drow = pair(*(e[0, pl.ds(8 + 2 * p + i, 1), :] for i in range(2)))
+            width = slots * TILE
+            peak = jnp.concatenate([st[0, pl.ds(2 * p + i, 1), pl.ds(0, width)] for i in range(2)], axis=1)
+            for n, (x, w) in enumerate(zip((vt, kt), probs_of(kp[p], kdp[p], peak, lrow, drow))):
+                if slots == 2:
+                    for i in range(2):
+                        d = pl.ds(pl.multiple_of(p * 128 + i * 64, 64), 64)
+                        ct[n, d, :] = dot_nn(x[i * 64 : (i + 1) * 64], w[:, i * 128 : (i + 1) * 128])
+                else:
+                    y = dot_nn(x, w)
+                    for i in range(2):
+                        d = pl.ds(pl.multiple_of(p * 128 + i * 64, 64), 64)
+                        ct[n, d, :] = dup_lanes(y[i * 64 : (i + 1) * 64], i)
+            return carry
+
+        lax.fori_loop(0, PAIRS, body, 0, unroll=True)
 
     def level_key(h, slots, e, c):
         n = slots * TILE
@@ -353,20 +378,42 @@
                 pr = jnp.exp2(sc[part] - stat_row(2 * p + i))
                 dss.append((pr * (dp[part] - stat_row(8 + 2 * p + i)) * SCALE).astype(BF16))
                 pbs.append(pr.astype(BF16))
-            c[2, :, cols] = sel2(dot_nn(jnp.concatenate(dss, axis=0), qq))
-            c[3, :, cols] = sel2(dot_nn(jnp.concatenate(pbs, axis=0), gg))
-            return carry
-
-        lax.fori_loop(0, PAIRS, body, 0)
-
-    def finish(outs):
+            c[0, :, cols] = sel2(dot_nn(jnp.concatenate(dss, axis=0), qq))
+            c[1, :, cols] = sel2(dot_nn(jnp.concatenate(pbs, axis=0), gg))
+            return carry
+
+        lax.fori_loop(0, PAIRS, body, 0, unroll=True)
+
+    def finish_query():
+        def body(p, carry):
+            cols = pl.ds(pl.multiple_of(p * 128, 128), 128)
+            first = lax.broadcasted_iota(jnp.int32, (128, 128), 0) < 64
+            right = lax.broadcasted_iota(jnp.int32, (128, 128), 1) // 64
+            pick_a = jnp.where(first, head(0, 2 * p), head(0, 2 * p + 1)) - right
+            pick_b = jnp.where(first, live_b(2 * p), live_b(2 * p + 1)) - right
+            pick_c = jnp.where(first, live_c(2 * p), live_c(2 * p + 1)) - right
+            for o in range(2):
+                a, b, c = cat[o, cols, :], cbt[o, cols, :], cct[o, cols, :]
+                for s in range(2):
+                    dup = dup_lanes(a, s)
+                    for t in range(2):
+                        j = 2 * s + t
+                        total = acct[o, cols, pl.ds(j * 128, 128)] + jnp.where(pick_a == 2 * t, dup, 0.0)
+                        total += jnp.where(pick_b == 2 * j, b, 0.0)
+                        total += jnp.where(pick_c == 2 * j, c, 0.0)
+                        stage[o, pl.ds(j * 128, 128), cols] = total.astype(BF16).T
+            return carry
+
+        lax.fori_loop(0, PAIRS, body, 0, unroll=True)
+
+    def finish_key():
         def body(p, carry):
             cols = pl.ds(pl.multiple_of(p * 128, 128), 128)
             low = low_lanes(TILE)
             pick_a = jnp.where(low, head(0, 2 * p), head(0, 2 * p + 1))
             pick_b = jnp.where(low, live_b(2 * p), live_b(2 * p + 1))
             pick_c = jnp.where(low, live_c(2 * p), live_c(2 * p + 1))
-            for o in outs:
+            for o in range(2):
                 b, c = cb[o, :, cols], cc[o, :, cols]
                 for t in range(8):
                     rows = pl.ds(t * TILE, TILE)
@@ -374,10 +421,10 @@
                     total = acc[o, rows, cols] + jnp.where(pick_a == t % 4, a, 0.0)
                     total += jnp.where(pick_b == t, b, 0.0)
                     total += jnp.where(pick_c == t, c, 0.0)
-                    stage[o, rows, cols] = total.astype(BF16)
-            return carry
-
-        lax.fori_loop(0, PAIRS, body, 0)
+                    stage[2 + o, rows, cols] = total.astype(BF16)
+            return carry
+
+        lax.fori_loop(0, PAIRS, body, 0, unroll=True)
 
     o_refs = (o_att, o_dq, o_dk, o_dv)
 
@@ -392,20 +439,26 @@
         return copies
 
     es = (ea, eb, ec)
-    for (h, slots, _, c), e in zip(levels, es):
-        level_query(h, slots, e, c)
-    finish((0, 1))
+    for (h, slots, st, c, ct, kp, kdp), e in zip(levels, es):
+        level_query(h, slots, st, ct, kp, kdp, e)
+    lax.fori_loop(0, 2 * PAIRS, local_back, 0, unroll=True)
+    finish_query()
     final = put((0, 1))
     waits = ((6, 7), (3, 6), (0, 3))
-    for (h, slots, _, c), e, (lo, hi) in zip(levels, es, waits):
+    for (h, slots, st, c, ct, kp, kdp), e, (lo, hi) in zip(levels, es, waits):
         for i in range(lo, hi):
             qg_copies[i].wait()
             x2[i].wait()
         level_key(h, slots, e, c)
-    finish((2, 3))
+    finish_key()
     final += put((2, 3))
     for c in final:
         c.wait()
+
+
+def hand_on(*refs):
+    for i in range(4):
+        refs[4 + i][...] = refs[i][...]
 
 
 def local(query_rows, key_rows, value_rows, grad_out, head_offset):
@@ -413,19 +466,27 @@
     any_spec = pl.BlockSpec(memory_space=pl.ANY)
     dma = pltpu.SemaphoreType.DMA
     tile4 = pltpu.VMEM((4, 4, TILE, HALF), BF16)
-    return pl.pallas_call(
+    results = pl.pallas_call(
         kernel,
         out_shape=[rows] * 4,
-        in_specs=[pl.BlockSpec(memory_space=pltpu.SMEM)] + [any_spec] * 4,
+        in_specs=[any_spec] * 5,
         out_specs=[any_spec] * 4,
         scratch_shapes=[pltpu.VMEM((2 * ROWS, HALF), BF16)] * 4
+        + [pltpu.VMEM((2, HALF, ROWS), BF16)] * 2
         + [tile4] * 3
         + [
-            pltpu.VMEM((4, 2 * ROWS, HALF), F32),
+            pltpu.VMEM((2, 2 * ROWS, HALF), F32),
+            pltpu.VMEM((2, HALF, 2 * ROWS), F32),
             pltpu.VMEM((4, 2 * ROWS, HALF), BF16),
-            pltpu.VMEM((4, 2 * TILE, HALF), F32),
-            pltpu.VMEM((4, TILE, HALF), F32),
-            pltpu.VMEM((4, TILE, HALF), F32),
+            pltpu.VMEM((2, 2 * TILE, HALF), F32),
+            pltpu.VMEM((2, TILE, HALF), F32),
+            pltpu.VMEM((2, TILE, HALF), F32),
+        ]
+        + [pltpu.VMEM((2, HALF, 128), F32)] * 3
+        + [pltpu.VMEM((2, PAIRS, ROWS, 2 * ROWS), F32)] * 2
+        + [pltpu.VMEM((PAIRS, ROWS, ROWS), F32)] * 2
+        + [pltpu.VMEM((PAIRS, ROWS, 128), F32)] * 4
+        + [
             pltpu.VMEM((3, 2, 8, ROWS), F32),
             pltpu.VMEM((3, 8, 128), F32),
             pltpu.VMEM((3, 8, 128), F32),
@@ -434,13 +495,20 @@
             pltpu.VMEM((2, 16, 128), F32),
             pltpu.VMEM((4, 16, 128), F32),
             pltpu.VMEM((4, 16, 128), F32),
+            pltpu.SMEM((3, HEADS), jnp.int32), dma(()),
             dma((4,)), dma((4,)), dma((4,)), dma((14,)), dma((14,)), dma((7,)), dma((7,)), dma((4,)), dma((4,)), dma((4,)),
         ],
         compiler_params=pltpu.CompilerParams(
-            collective_id=0, has_side_effects=True, vmem_limit_bytes=40 * 1024 * 1024
+            collective_id=0, has_side_effects=True, vmem_limit_bytes=64 * 1024 * 1024
         ),
         cost_estimate=pl.CostEstimate(flops=2_000_000_000, bytes_accessed=3_200_000, transcendentals=3_000_000),
     )(head_offset, query_rows, key_rows, value_rows, grad_out)
+    return pl.pallas_call(
+        hand_on,
+        out_shape=[rows] * 4,
+        in_specs=[pl.BlockSpec(memory_space=pltpu.VMEM)] * 4,
+        out_specs=[pl.BlockSpec(memory_space=pltpu.VMEM)] * 4,
+    )(*results)
 
 
 def solution(mesh):

time: 52.4 us -> 40 us (0.76)
  local copies, waits for them, and re-layouts: 7.64 us -> 0 us
  Pallas kernels: 43.9 us -> 39.2 us
    unnamed x14 -> x0, local copies, waits for them, and re-layouts: 7.64 us -> none
    pallas_call x1 -> x2, Pallas kernels: 43.9 us -> 39.2 us  [the longest x1 36.7 us: local(): pl.pallas_call(kernel, out_shape=[rows] * 4, in_specs=[any_spec] * 5, out...]
where the time goes in v1:
time: 40 us; the launch traced here: 39.9 us
  Pallas kernels  39.2 us (98%)
  between operations  0.64 us (2%)
    pallas_call x1, Pallas kernels, local(): pl.pallas_call(kernel, out_shape=[rows] * 4, in_specs=[any_spec] * 5, out...  36.7 us
    pallas_call x1, Pallas kernels, local(): pl.pallas_call(hand_on, out_shape=[rows] * 4, in_specs=[pl.BlockSpec(memo...  2.51 us

profile of v1, /device:TPU:1, one launch (start us, length us, event | category | flops | bytes accessed | tf_op | source)
XLA Modules:
  0.0 39.9 jit_solution(9889390459420679123)
XLA Ops:
  0.6 36.7 %shard_map.84 = (bf16[256,768]{1,0:T(8,128)(2,1)}, bf16[256,768]{1,0:T(8,128)(2,1)}, bf16[256,768]{1,0:T(8,128)(2,1)}, bf16[256,768]{1,0:T(8,128)(2,1)}) custom-call(s32[3,12]{1,0:T(4,128)} %off_hbm.1, bf16[256,768]{1,0:T(8,128)(2,1)} %q_hbm.1, bf16[256,768]{1,0:T(8,128)(2,1)} %k_hbm.1, bf16[256,768]{1,0:T(8,128)(2,1)} %v_hbm.1, bf16[256,768]{1,0:T(8,128)(2,1)} %g_hbm.1), custom_call_target="tpu_custom_call" | custom-call | flops 2000000000 | bytes 3200000 | tf_op jit(solution)/shard_map/pallas_call | solution.py:469
  37.3 2.5 %shard_map.85 = (bf16[256,768]{1,0:T(8,128)(2,1)}, bf16[256,768]{1,0:T(8,128)(2,1)}, bf16[256,768]{1,0:T(8,128)(2,1)}, bf16[256,768]{1,0:T(8,128)(2,1)}) custom-call(bf16[256,768]{1,0:T(8,128)(2,1)} %get-tuple-element.8.refs_0_, bf16[256,768]{1,0:T(8,128)(2,1)} %get-tuple-element.9.refs_1_, bf16[256,768]{1,0:T(8,128)(2,1)} %get-tuple-element.10.refs_2_, ...), custom_call_target="tpu_custom_call" | custom-call | tf_op jit(solution)/shard_map/pallas_call | solution.py:506

commit v2 on v1

--- a/solution.py
+++ b/solution.py
@@ -137,10 +137,6 @@
         for st in (sta, stb, stc):
             st[n] = zero8[:, :128]
 
-    for c in loads:
-        c.wait()
-    load_off.wait()
-    local_stats(core)
     pl.semaphore_wait(barrier, len(masks))
 
     def remote(src, dst, send, recv, mask):
@@ -185,30 +181,54 @@
 
         lax.fori_loop(0, PAIRS, body, 0, unroll=True)
 
-    def send_tiles(half):
-        two = pl.ds(2 * half, 2)
-        base = 7 * half
-        copies = []
-        for i, m in enumerate(MASK_C):
-            copies.append(remote(hc.at[two, 0], hc.at[two, i + 1], x1_send.at[base + i], x1_recv.at[base + i], m))
-        for i, m in enumerate(MASK_B):
-            copies.append(remote(hb.at[two, 0], hb.at[two, i + 1], x1_send.at[base + 3 + i], x1_recv.at[base + 3 + i], m))
-        copies.append(
-            remote(ha.at[two, pl.ds(0, 2)], ha.at[two, pl.ds(2, 2)], x1_send.at[base + 6], x1_recv.at[base + 6], MASK_A[0])
-        )
-        for c in copies:
-            c.start()
-        return copies
-
+    keys, queries = pl.ds(0, 2), pl.ds(2, 2)
+
+    def tiles(h, arrays, src, dst, sem, mask):
+        return remote(h.at[arrays, src], h.at[arrays, dst], x1_send.at[sem], x1_recv.at[sem], mask)
+
+    kv_c1 = tiles(hc, keys, 0, 1, 0, 64)
+    kv_c3 = tiles(hc, keys, 0, 3, 1, 192)
+    kv_b1 = tiles(hb, keys, 0, 1, 2, 4)
+    kv_b2 = tiles(hb, keys, 0, 2, 3, 8)
+    kv_a = tiles(ha, keys, pl.ds(0, 2), pl.ds(2, 2), 4, 2)
+    relay_k = tiles(hc, 0, 3, 2, 5, 64)
+    relay_v = tiles(hc, 1, 1, 2, 6, 192)
+    relay_b = tiles(hb, keys, 1, 3, 7, 8)
+    qg_c1 = tiles(hc, queries, 0, 1, 8, 64)
+    qg_c3 = tiles(hc, queries, 0, 3, 9, 192)
+    qg_b1 = tiles(hb, queries, 0, 1, 10, 4)
+    qg_b2 = tiles(hb, queries, 0, 2, 11, 8)
+    qg_a = tiles(ha, queries, pl.ds(0, 2), pl.ds(2, 2), 12, 2)
+    relay_q = tiles(hc, 2, 3, 2, 13, 64)
+    relay_g = tiles(hc, 3, 1, 2, 14, 192)
+    relay_qb = tiles(hb, queries, 1, 3, 15, 8)
+
+    loads[0].wait()
+    loads[1].wait()
+    load_off.wait()
     s1[0].wait()
     s1[1].wait()
     pick(0)
-    kv_copies = send_tiles(0)
+    for c in (kv_c1, kv_c3, kv_b1, kv_b2):
+        c.start()
     s1[2].wait()
     s1[3].wait()
+    loads[2].wait()
+    loads[3].wait()
     pick(2)
-    qg_copies = send_tiles(1)
+    kv_b1.wait_send()
+    kv_b2.wait_send()
+    kv_a.start()
+    local_stats(core)
+    kv_c1.wait_send()
+    kv_c3.wait_send()
+    for c in (qg_c1, qg_c3, qg_b1, qg_b2):
+        c.start()
+    kv_b1.wait_recv()
+    relay_b.start()
     local_stats(other)
+    kv_a.wait_send()
+    qg_a.start()
 
     levels = ((ha, 2, sta, ca, cat, ap, adp), (hb, 1, stb, cb, cbt, bp, bdp), (hc, 1, stc, cc, cct, cp, cdp))
 
@@ -234,13 +254,23 @@
 
         lax.fori_loop(0, PAIRS, body, 0, unroll=True)
 
-    kv_copies[6].wait()
+    kv_c3.wait_recv()
+    relay_k.start()
+    kv_c1.wait_recv()
+    relay_v.start()
+    kv_a.wait_recv()
     level_stats(*levels[0])
-    for c in kv_copies[3:6]:
-        c.wait()
+    kv_b2.wait_recv()
+    relay_b.wait()
     level_stats(*levels[1])
-    for c in kv_copies[:3]:
-        c.wait()
+    qg_b1.wait()
+    relay_qb.start()
+    qg_c3.wait()
+    relay_q.start()
+    qg_c1.wait()
+    relay_g.start()
+    relay_k.wait()
+    relay_v.wait()
     level_stats(*levels[2])
 
     row_id = lax.broadcasted_iota(jnp.int32, (8, ROWS), 0)
@@ -406,21 +436,32 @@
 
         lax.fori_loop(0, PAIRS, body, 0, unroll=True)
 
-    def finish_key():
+    def finish_near():
         def body(p, carry):
             cols = pl.ds(pl.multiple_of(p * 128, 128), 128)
             low = low_lanes(TILE)
             pick_a = jnp.where(low, head(0, 2 * p), head(0, 2 * p + 1))
             pick_b = jnp.where(low, live_b(2 * p), live_b(2 * p + 1))
-            pick_c = jnp.where(low, live_c(2 * p), live_c(2 * p + 1))
             for o in range(2):
-                b, c = cb[o, :, cols], cc[o, :, cols]
+                b = cb[o, :, cols]
                 for t in range(8):
                     rows = pl.ds(t * TILE, TILE)
                     a = ca[o, pl.ds(t // 4 * TILE, TILE), cols]
                     total = acc[o, rows, cols] + jnp.where(pick_a == t % 4, a, 0.0)
-                    total += jnp.where(pick_b == t, b, 0.0)
-                    total += jnp.where(pick_c == t, c, 0.0)
+                    acc[o, rows, cols] = total + jnp.where(pick_b == t, b, 0.0)
+            return carry
+
+        lax.fori_loop(0, PAIRS, body, 0, unroll=True)
+
+    def finish_key():
+        def body(p, carry):
+            cols = pl.ds(pl.multiple_of(p * 128, 128), 128)
+            pick_c = jnp.where(low_lanes(TILE), live_c(2 * p), live_c(2 * p + 1))
+            for o in range(2):
+                c = cc[o, :, cols]
+                for t in range(8):
+                    rows = pl.ds(t * TILE, TILE)
+                    total = acc[o, rows, cols] + jnp.where(pick_c == t, c, 0.0)
                     stage[2 + o, rows, cols] = total.astype(BF16)
             return carry
 
@@ -444,11 +485,12 @@
     lax.fori_loop(0, 2 * PAIRS, local_back, 0, unroll=True)
     finish_query()
     final = put((0, 1))
-    waits = ((6, 7), (3, 6), (0, 3))
-    for (h, slots, st, c, ct, kp, kdp), e, (lo, hi) in zip(levels, es, waits):
-        for i in range(lo, hi):
-            qg_copies[i].wait()
-            x2[i].wait()
+    x2_of = (x2[6:], x2[3:6], x2[:3])
+    for (h, slots, st, c, ct, kp, kdp), e, tile_copies, row_copies in zip(levels, es, ([qg_a], [qg_b2, relay_qb], [relay_q, relay_g]), x2_of):
+        if h is hc:
+            finish_near()
+        for copy in tile_copies + row_copies:
+            copy.wait()
         level_key(h, slots, e, c)
     finish_key()
     final += put((2, 3))
@@ -457,8 +499,16 @@
 
 
 def hand_on(*refs):
-    for i in range(4):
-        refs[4 + i][...] = refs[i][...]
+    ins, outs, (held, in_sem, out_sem) = refs[:4], refs[4:8], refs[8:]
+    loads = [pltpu.make_async_copy(ins[i], held.at[i], in_sem.at[i]) for i in range(4)]
+    stores = [pltpu.make_async_copy(held.at[i], outs[i], out_sem.at[i]) for i in range(4)]
+    for c in loads:
+        c.start()
+    for load, store in zip(loads, stores):
+        load.wait()
+        store.start()
+    for c in stores:
+        c.wait()
 
 
 def local(query_rows, key_rows, value_rows, grad_out, head_offset):
@@ -496,7 +546,7 @@
             pltpu.VMEM((4, 16, 128), F32),
             pltpu.VMEM((4, 16, 128), F32),
             pltpu.SMEM((3, HEADS), jnp.int32), dma(()),
-            dma((4,)), dma((4,)), dma((4,)), dma((14,)), dma((14,)), dma((7,)), dma((7,)), dma((4,)), dma((4,)), dma((4,)),
+            dma((4,)), dma((4,)), dma((4,)), dma((16,)), dma((16,)), dma((7,)), dma((7,)), dma((4,)), dma((4,)), dma((4,)),
         ],
         compiler_params=pltpu.CompilerParams(
             collective_id=0, has_side_effects=True, vmem_limit_bytes=64 * 1024 * 1024
@@ -506,8 +556,10 @@
     return pl.pallas_call(
         hand_on,
         out_shape=[rows] * 4,
-        in_specs=[pl.BlockSpec(memory_space=pltpu.VMEM)] * 4,
-        out_specs=[pl.BlockSpec(memory_space=pltpu.VMEM)] * 4,
+        in_specs=[any_spec] * 4,
+        out_specs=[any_spec] * 4,
+        scratch_shapes=[pltpu.VMEM((4, ROWS, 2 * HALF), BF16), dma((4,)), dma((4,))],
+        compiler_params=pltpu.CompilerParams(vmem_limit_bytes=64 * 1024 * 1024),
     )(*results)
 
 

time: 40 us -> 37 us (0.925)
  Pallas kernels: 39.2 us -> 36.3 us
    pallas_call x1, Pallas kernels: 36.7 us -> 34.1 us  [local(): pl.pallas_call(kernel, out_shape=[rows] * 4, in_specs=[any_spec] * 5, out...]
where the time goes in v2:
time: 37 us; the launch traced here: 36.9 us
  Pallas kernels  36.3 us (98%)
  between operations  0.64 us (2%)
    pallas_call x1, Pallas kernels, local(): pl.pallas_call(kernel, out_shape=[rows] * 4, in_specs=[any_spec] * 5, out...  34.1 us
    pallas_call x1, Pallas kernels, local(): pl.pallas_call(hand_on, out_shape=[rows] * 4, in_specs=[any_spec] * 4, ou...  2.2 us

profile of v2, /device:TPU:1, one launch (start us, length us, event | category | flops | bytes accessed | tf_op | source)
XLA Modules:
  0.0 36.9 jit_solution(7886742320935085770)
XLA Ops:
  0.6 34.1 %shard_map.84 = (bf16[256,768]{1,0:T(8,128)(2,1)}, bf16[256,768]{1,0:T(8,128)(2,1)}, bf16[256,768]{1,0:T(8,128)(2,1)}, bf16[256,768]{1,0:T(8,128)(2,1)}) custom-call(s32[3,12]{1,0:T(4,128)} %off_hbm.1, bf16[256,768]{1,0:T(8,128)(2,1)} %q_hbm.1, bf16[256,768]{1,0:T(8,128)(2,1)} %k_hbm.1, bf16[256,768]{1,0:T(8,128)(2,1)} %v_hbm.1, bf16[256,768]{1,0:T(8,128)(2,1)} %g_hbm.1), custom_call_target="tpu_custom_call" | custom-call | flops 2000000000 | bytes 3200000 | tf_op jit(solution)/shard_map/pallas_call | solution.py:519
  34.7 2.2 %shard_map.85 = (bf16[256,768]{1,0:T(8,128)(2,1)}, bf16[256,768]{1,0:T(8,128)(2,1)}, bf16[256,768]{1,0:T(8,128)(2,1)}, bf16[256,768]{1,0:T(8,128)(2,1)}) custom-call(bf16[256,768]{1,0:T(8,128)(2,1)} %get-tuple-element.8.refs_0_, bf16[256,768]{1,0:T(8,128)(2,1)} %get-tuple-element.9.refs_1_, bf16[256,768]{1,0:T(8,128)(2,1)} %get-tuple-element.10.refs_2_, ...), custom_call_target="tpu_custom_call" | custom-call | tf_op jit(solution)/shard_map/pallas_call | solution.py:556

commit v3 on v2

--- a/solution.py
+++ b/solution.py
@@ -152,7 +152,7 @@
     for c in s1:
         c.start()
 
-    def pick(first):
+    def pick(*arrays):
         def body(p, carry):
             cols = pl.ds(pl.multiple_of(p * 128, 128), 128)
             low = lax.broadcasted_iota(jnp.int32, (1, 128), 1) < 64
@@ -171,7 +171,7 @@
                     out += tile * one
                 return out
 
-            for n in (first, first + 1):
+            for n in arrays:
                 tiles = [xs[n][pl.ds(t * TILE, TILE), cols] for t in range(8)]
                 hc[n, 0, :, cols] = mix(tiles, hot_c)
                 hb[n, 0, :, cols] = mix(tiles, hot_b)
@@ -186,49 +186,59 @@
     def tiles(h, arrays, src, dst, sem, mask):
         return remote(h.at[arrays, src], h.at[arrays, dst], x1_send.at[sem], x1_recv.at[sem], mask)
 
-    kv_c1 = tiles(hc, keys, 0, 1, 0, 64)
-    kv_c3 = tiles(hc, keys, 0, 3, 1, 192)
-    kv_b1 = tiles(hb, keys, 0, 1, 2, 4)
-    kv_b2 = tiles(hb, keys, 0, 2, 3, 8)
-    kv_a = tiles(ha, keys, pl.ds(0, 2), pl.ds(2, 2), 4, 2)
-    relay_k = tiles(hc, 0, 3, 2, 5, 64)
-    relay_v = tiles(hc, 1, 1, 2, 6, 192)
-    relay_b = tiles(hb, keys, 1, 3, 7, 8)
-    qg_c1 = tiles(hc, queries, 0, 1, 8, 64)
-    qg_c3 = tiles(hc, queries, 0, 3, 9, 192)
-    qg_b1 = tiles(hb, queries, 0, 1, 10, 4)
-    qg_b2 = tiles(hb, queries, 0, 2, 11, 8)
-    qg_a = tiles(ha, queries, pl.ds(0, 2), pl.ds(2, 2), 12, 2)
-    relay_q = tiles(hc, 2, 3, 2, 13, 64)
-    relay_g = tiles(hc, 3, 1, 2, 14, 192)
-    relay_qb = tiles(hb, queries, 1, 3, 15, 8)
-
+    up = [tiles(hc, n, 0, 1, n, 64) for n in range(4)]
+    down = [tiles(hc, n, 0, 3, 4 + n, 192) for n in range(4)]
+    relay_k, relay_q = (tiles(hc, n, 3, 2, 8 + n, 64) for n in (0, 2))
+    relay_v, relay_g = (tiles(hc, n, 1, 2, 8 + n, 192) for n in (1, 3))
+    kv_b1 = tiles(hb, keys, 0, 1, 12, 4)
+    kv_b2 = tiles(hb, keys, 0, 2, 13, 8)
+    kv_a = tiles(ha, keys, pl.ds(0, 2), pl.ds(2, 2), 14, 2)
+    relay_b = tiles(hb, keys, 1, 3, 15, 8)
+    qg_b1 = tiles(hb, queries, 0, 1, 16, 4)
+    qg_b2 = tiles(hb, queries, 0, 2, 17, 8)
+    qg_a = tiles(ha, queries, pl.ds(0, 2), pl.ds(2, 2), 18, 2)
+    relay_qb = tiles(hb, queries, 1, 3, 19, 8)
+
+    load_off.wait()
     loads[0].wait()
+    s1[0].wait()
+    pick(0)
+    down[0].start()
     loads[1].wait()
-    load_off.wait()
-    s1[0].wait()
     s1[1].wait()
-    pick(0)
-    for c in (kv_c1, kv_c3, kv_b1, kv_b2):
+    pick(1)
+    for c in (up[1], kv_b1, kv_b2):
         c.start()
-    s1[2].wait()
-    s1[3].wait()
-    loads[2].wait()
-    loads[3].wait()
-    pick(2)
+    for c in loads[2:] + s1[2:]:
+        c.wait()
+    pick(2, 3)
+    down[0].wait_send()
+    down[1].start()
+    up[1].wait_send()
+    up[0].start()
     kv_b1.wait_send()
     kv_b2.wait_send()
     kv_a.start()
     local_stats(core)
-    kv_c1.wait_send()
-    kv_c3.wait_send()
-    for c in (qg_c1, qg_c3, qg_b1, qg_b2):
-        c.start()
+    down[1].wait_send()
+    down[2].start()
+    up[0].wait_send()
+    up[3].start()
+    qg_b1.start()
+    qg_b2.start()
     kv_b1.wait_recv()
     relay_b.start()
+    down[0].wait_recv()
+    relay_k.start()
+    up[1].wait_recv()
+    relay_v.start()
     local_stats(other)
     kv_a.wait_send()
     qg_a.start()
+    down[2].wait_send()
+    down[3].start()
+    up[3].wait_send()
+    up[2].start()
 
     levels = ((ha, 2, sta, ca, cat, ap, adp), (hb, 1, stb, cb, cbt, bp, bdp), (hc, 1, stc, cc, cct, cp, cdp))
 
@@ -254,24 +264,22 @@
 
         lax.fori_loop(0, PAIRS, body, 0, unroll=True)
 
-    kv_c3.wait_recv()
-    relay_k.start()
-    kv_c1.wait_recv()
-    relay_v.start()
     kv_a.wait_recv()
     level_stats(*levels[0])
     kv_b2.wait_recv()
     relay_b.wait()
     level_stats(*levels[1])
-    qg_b1.wait()
-    relay_qb.start()
-    qg_c3.wait()
-    relay_q.start()
-    qg_c1.wait()
-    relay_g.start()
+    down[1].wait_recv()
+    up[0].wait_recv()
     relay_k.wait()
     relay_v.wait()
     level_stats(*levels[2])
+    qg_b1.wait()
+    relay_qb.start()
+    down[2].wait_recv()
+    relay_q.start()
+    up[3].wait_recv()
+    relay_g.start()
 
     row_id = lax.broadcasted_iota(jnp.int32, (8, ROWS), 0)
     lane_tile = lax.broadcasted_iota(jnp.int32, (8, ROWS), 1) // TILE
@@ -491,6 +499,9 @@
             finish_near()
         for copy in tile_copies + row_copies:
             copy.wait()
+        if h is hc:
+            down[3].wait()
+            up[2].wait()
         level_key(h, slots, e, c)
     finish_key()
     final += put((2, 3))
@@ -546,7 +557,7 @@
             pltpu.VMEM((4, 16, 128), F32),
             pltpu.VMEM((4, 16, 128), F32),
             pltpu.SMEM((3, HEADS), jnp.int32), dma(()),
-            dma((4,)), dma((4,)), dma((4,)), dma((16,)), dma((16,)), dma((7,)), dma((7,)), dma((4,)), dma((4,)), dma((4,)),
+            dma((4,)), dma((4,)), dma((4,)), dma((20,)), dma((20,)), dma((7,)), dma((7,)), dma((4,)), dma((4,)), dma((4,)),
         ],
         compiler_params=pltpu.CompilerParams(
             collective_id=0, has_side_effects=True, vmem_limit_bytes=64 * 1024 * 1024

time: 37 us -> 36.1 us (0.976)
  Pallas kernels: 36.3 us -> 35.3 us
    pallas_call x1, Pallas kernels: 34.1 us -> 33.1 us  [local(): pl.pallas_call(kernel, out_shape=[rows] * 4, in_specs=[any_spec] * 5, out...]
where the time goes in v3:
time: 36.1 us; the launch traced here: 36 us
  Pallas kernels  35.3 us (98%)
  between operations  0.64 us (2%)
    pallas_call x1, Pallas kernels, local(): pl.pallas_call(kernel, out_shape=[rows] * 4, in_specs=[any_spec] * 5, out...  33.1 us
    pallas_call x1, Pallas kernels, local(): pl.pallas_call(hand_on, out_shape=[rows] * 4, in_specs=[any_spec] * 4, ou...  2.2 us

profile of v3, /device:TPU:1, one launch (start us, length us, event | category | flops | bytes accessed | tf_op | source)
XLA Modules:
  0.0 36.0 jit_solution(1420281539208334313)
XLA Ops:
  0.6 33.1 %shard_map.84 = (bf16[256,768]{1,0:T(8,128)(2,1)}, bf16[256,768]{1,0:T(8,128)(2,1)}, bf16[256,768]{1,0:T(8,128)(2,1)}, bf16[256,768]{1,0:T(8,128)(2,1)}) custom-call(s32[3,12]{1,0:T(4,128)} %off_hbm.1, bf16[256,768]{1,0:T(8,128)(2,1)} %q_hbm.1, bf16[256,768]{1,0:T(8,128)(2,1)} %k_hbm.1, bf16[256,768]{1,0:T(8,128)(2,1)} %v_hbm.1, bf16[256,768]{1,0:T(8,128)(2,1)} %g_hbm.1), custom_call_target="tpu_custom_call" | custom-call | flops 2000000000 | bytes 3200000 | tf_op jit(solution)/shard_map/pallas_call | solution.py:530
  33.8 2.2 %shard_map.85 = (bf16[256,768]{1,0:T(8,128)(2,1)}, bf16[256,768]{1,0:T(8,128)(2,1)}, bf16[256,768]{1,0:T(8,128)(2,1)}, bf16[256,768]{1,0:T(8,128)(2,1)}) custom-call(bf16[256,768]{1,0:T(8,128)(2,1)} %get-tuple-element.8.refs_0_, bf16[256,768]{1,0:T(8,128)(2,1)} %get-tuple-element.9.refs_1_, bf16[256,768]{1,0:T(8,128)(2,1)} %get-tuple-element.10.refs_2_, ...), custom_call_target="tpu_custom_call" | custom-call | tf_op jit(solution)/shard_map/pallas_call | solution.py:567

commit v4 on v3

--- a/solution.py
+++ b/solution.py
@@ -149,8 +149,8 @@
         remote(h.at[:, sib_cols], x.at[my_rows, :], s1_send.at[i], s1_recv.at[i], SIB)
         for i, (h, x) in enumerate(zip(hbm, xs))
     ]
-    for c in s1:
-        c.start()
+    s1[0].start()
+    s1[1].start()
 
     def pick(*arrays):
         def body(p, carry):
@@ -202,10 +202,12 @@
     load_off.wait()
     loads[0].wait()
     s1[0].wait()
+    s1[2].start()
     pick(0)
     down[0].start()
     loads[1].wait()
     s1[1].wait()
+    s1[3].start()
     pick(1)
     for c in (up[1], kv_b1, kv_b2):
         c.start()

time: 36.1 us -> 35.7 us (0.989)
  Pallas kernels: 35.3 us -> 34.9 us
    pallas_call x1, Pallas kernels: 33.1 us -> 32.7 us  [local(): pl.pallas_call(kernel, out_shape=[rows] * 4, in_specs=[any_spec] * 5, out...]
where the time goes in v4:
time: 35.7 us; the launch traced here: 35.6 us
  Pallas kernels  34.9 us (98%)
  between operations  0.64 us (2%)
    pallas_call x1, Pallas kernels, local(): pl.pallas_call(kernel, out_shape=[rows] * 4, in_specs=[any_spec] * 5, out...  32.7 us
    pallas_call x1, Pallas kernels, local(): pl.pallas_call(hand_on, out_shape=[rows] * 4, in_specs=[any_spec] * 4, ou...  2.2 us

profile of v4, /device:TPU:1, one launch (start us, length us, event | category | flops | bytes accessed | tf_op | source)
XLA Modules:
  0.0 35.6 jit_solution(14781610371371707112)
XLA Ops:
  0.6 32.7 %shard_map.84 = (bf16[256,768]{1,0:T(8,128)(2,1)}, bf16[256,768]{1,0:T(8,128)(2,1)}, bf16[256,768]{1,0:T(8,128)(2,1)}, bf16[256,768]{1,0:T(8,128)(2,1)}) custom-call(s32[3,12]{1,0:T(4,128)} %off_hbm.1, bf16[256,768]{1,0:T(8,128)(2,1)} %q_hbm.1, bf16[256,768]{1,0:T(8,128)(2,1)} %k_hbm.1, bf16[256,768]{1,0:T(8,128)(2,1)} %v_hbm.1, bf16[256,768]{1,0:T(8,128)(2,1)} %g_hbm.1), custom_call_target="tpu_custom_call" | custom-call | flops 2000000000 | bytes 3200000 | tf_op jit(solution)/shard_map/pallas_call | solution.py:532
  33.4 2.2 %shard_map.85 = (bf16[256,768]{1,0:T(8,128)(2,1)}, bf16[256,768]{1,0:T(8,128)(2,1)}, bf16[256,768]{1,0:T(8,128)(2,1)}, bf16[256,768]{1,0:T(8,128)(2,1)}) custom-call(bf16[256,768]{1,0:T(8,128)(2,1)} %get-tuple-element.8.refs_0_, bf16[256,768]{1,0:T(8,128)(2,1)} %get-tuple-element.9.refs_1_, bf16[256,768]{1,0:T(8,128)(2,1)} %get-tuple-element.10.refs_2_, ...), custom_call_target="tpu_custom_call" | custom-call | tf_op jit(solution)/shard_map/pallas_call | solution.py:569
